TPU v7x, 256 devices: a whole 4x4x8 slice. The times are simulated.
256 devices in a mesh: dom: 64 (over z, y, core), local: 4 (over x).
Axes of the slice: x: 4, y: 4, z: 8, core: 2. Of those that a mesh axis runs over, the one named last changes fastest.
Arguments:
- features: bfloat16 [1048576, 256], P(('dom', 'local')), may hold values from -6 to 6
- w_self: bfloat16 [256, 128], replicated, may hold values from -0.375 to 0.375
- w_neigh: bfloat16 [256, 128], replicated, may hold values from -0.375 to 0.375
- bias_vector: float32 [128], replicated, may hold values from -3 to 3
- adjacency: bfloat16 [49152, 128, 128], P(('dom', 'local')), may hold values from 0 to 1, as said below
- tile_at: int32 [49152, 2], P(('dom', 'local')), may hold values from 0 to 47, as said below
- clone_root: int32 [256, 256, 8], P(('dom', 'local')), may hold values from 0 to 4095, as said below
- clone_count: int32 [256, 256], P(('dom', 'local')), may hold values from 1 to 8, as said below
- degrees: int32 [1048576], P(('dom', 'local')), may hold values from 16 to 63
- cotangent: bfloat16 [1048576, 128], P(('dom', 'local')), may hold values from -6 to 6
Outputs:
- activation: bfloat16 [1048576, 128], P(('dom', 'local'))
- grad_features: bfloat16 [1048576, 256], P(('dom', 'local'))
- grad_self: float32 [256, 128], replicated
- grad_neigh: float32 [256, 128], replicated
Inputs may be any that keep to these rules, and one draw needn't show every extreme that they name: `adjacency`: entries are 0 or 1. `tile_at`: column 0 is a tile's destination block among the device's slot rows, column 1 its source block among the device's own nodes; every destination block of a device is named by at least one of its tiles. `clone_root`: the live entries of one bucket (e, d) are distinct. Every device e has some sender d with clone_count[e, d] = 8.
All inputs are finite; a program needn't handle non-finite values.
Results may differ from a plain program's by a relative error of at most 0.0052.
Values may be sent and summed in bfloat16 or wider, within the bound.
A program may use at most 128 MiB of HBM per device.

v0:
```python
import jax
import jax.numpy as jnp
from jax import lax
from jax.sharding import PartitionSpec as P

BLOCK = 128


def per_device(
    features,
    w_self,
    w_neigh,
    bias_vector,
    adjacency,
    tile_at,
    clone_root,
    clone_count,
    degrees,
    cotangent,
):
    root_rows = features.shape[0]
    out_width = w_neigh.shape[1]
    dom_count = lax.axis_size("dom")
    local_count = lax.axis_size("local")
    device_total = dom_count * local_count
    capacity = clone_root.shape[2]
    clone_rows = device_total * capacity
    dest_blocks = (root_rows + clone_rows) // BLOCK
    source_blocks = root_rows // BLOCK
    dest_block = tile_at[:, 0]
    source_block = tile_at[:, 1]
    projected = jnp.dot(features, w_neigh, preferred_element_type=jnp.float32).astype(jnp.bfloat16)
    picked = projected.reshape(source_blocks, BLOCK, out_width)[source_block]
    products = jnp.einsum("tij,tjf->tif", adjacency, picked, preferred_element_type=jnp.float32)
    partial_value = jax.ops.segment_sum(products, dest_block, num_segments=dest_blocks)
    partial_value = partial_value.reshape(root_rows + clone_rows, out_width)
    outgoing = (
        partial_value[root_rows:]
        .astype(jnp.bfloat16)
        .reshape(dom_count, local_count, capacity, out_width)
    )
    own_term = jnp.dot(features, w_self, preferred_element_type=jnp.float32) + bias_vector[None, :]
    arrived = lax.all_to_all(
        lax.all_to_all(outgoing, "local", split_axis=1, concat_axis=1, tiled=True),
        "dom",
        split_axis=0,
        concat_axis=0,
        tiled=True,
    )
    counts = clone_count[0]
    targets = clone_root[0].reshape(clone_rows)
    is_live = jnp.arange(capacity, dtype=jnp.int32)[None, :] < counts[:, None]
    arrived_f = arrived.astype(jnp.float32).reshape(device_total, capacity, out_width)
    incoming = jnp.where(is_live[:, :, None], arrived_f, jnp.zeros((), jnp.float32))
    total = partial_value[:root_rows].at[targets].add(incoming.reshape(clone_rows, out_width))
    degree_f = degrees.astype(jnp.float32)[:, None]
    preact = own_term + total / degree_f
    sigmoid_val = jax.nn.sigmoid(preact)
    activation = (preact * sigmoid_val).astype(jnp.bfloat16)
    grad_full = cotangent.astype(jnp.float32) * sigmoid_val * (1.0 + preact * (1.0 - sigmoid_val))
    grad_pre = grad_full.astype(jnp.bfloat16)
    grad_mean = (grad_full / degree_f).astype(jnp.bfloat16)
    returned = grad_mean[targets].reshape(device_total, capacity, out_width)
    returned = jnp.where(is_live[:, :, None], returned, jnp.zeros((), jnp.bfloat16))
    returned = returned.reshape(dom_count, local_count, capacity, out_width)
    scale_factor = float(root_rows * device_total) ** (-0.5)
    contract_rows = (((0,), (0,)), ((), ()))
    back = lax.all_to_all(
        lax.all_to_all(returned, "local", split_axis=1, concat_axis=1, tiled=True),
        "dom",
        split_axis=0,
        concat_axis=0,
        tiled=True,
    )
    slot_grad = jnp.concatenate([grad_mean, back.reshape(clone_rows, out_width)], axis=0)
    dest_rows = slot_grad.reshape(dest_blocks, BLOCK, out_width)[dest_block]
    back_products = jnp.einsum(
        "tij,tif->tjf", adjacency, dest_rows, preferred_element_type=jnp.float32
    )
    grad_proj = jax.ops.segment_sum(back_products, source_block, num_segments=source_blocks)
    grad_proj = grad_proj.reshape(root_rows, out_width).astype(jnp.bfloat16)
    grad_features = (
        jnp.dot(grad_pre, w_self.T, preferred_element_type=jnp.float32)
        + jnp.dot(grad_proj, w_neigh.T, preferred_element_type=jnp.float32)
    ).astype(jnp.bfloat16)
    joined = jnp.concatenate([grad_pre, grad_proj], axis=1)
    both_terms = (
        lax.dot_general(features, joined, contract_rows, preferred_element_type=jnp.float32)
        * scale_factor
    )
    summed = lax.psum(both_terms, ("dom", "local"))
    grad_self = summed[:, :out_width]
    grad_neigh = summed[:, out_width:]
    return (activation, grad_features, grad_self, grad_neigh)


def solution(mesh):
    placed = (
        P(("dom", "local"), None),
        P(),
        P(),
        P(),
        P(("dom", "local"), None, None),
        P(("dom", "local"), None),
        P(("dom", "local"), None, None),
        P(("dom", "local"), None),
        P(("dom", "local")),
        P(("dom", "local"), None),
    )
    return jax.shard_map(
        per_device,
        mesh=mesh,
        in_specs=placed,
        out_specs=(P(("dom", "local"), None), P(("dom", "local"), None), P(), P()),
        check_vma=False,
    )
```

profile of v0, /device:TPU:1, one launch (start us, length us, event | category | flops | bytes accessed | tf_op | source)
XLA Modules:
  0.0 530.4 jit_solution(15069269810759278203)
XLA Ops:
  10.3 8.0 %gather_fusion = bf16[192,128,128]{2,1,0:T(8,128)(2,1)} fusion(bf16[32,128,128]{2,1,0:T(8,128)(2,1)S(1)} %bitcast.34, s32[1024]{0:T(1024)S(1)} %pad_clamp_fusion.1), kind=kCustom, calls=%fused_computation | custom fusion | bytes 12583680 | tf_op jit(solution)/shard_map/gather | solution.py:33
  18.4 13.6 %convolution_bitcast_fusion.1 = f32[192,128,128]{1,2,0:T(8,128)} fusion(bf16[192,128,128]{2,1,0:T(8,128)(2,1)} %gather_fusion, bf16[192,128,128]{2,1,0:T(8,128)(2,1)} %param.14), kind=kOutput, calls=%fused_computation.12 | convolution fusion | flops 805306368 | bytes 25165824 | tf_op jit(solution)/shard_map/tij,tjf->tif/dot_general | solution.py:34
  32.0 12.6 %copy.38 = f32[192,128,128]{2,1,0:T(8,128)} copy(f32[192,128,128]{1,2,0:T(8,128)} %convolution_bitcast_fusion.1) | data formatting | bytes 25165824 | tf_op jit(solution)/shard_map/tij,tjf->tif/dot_general | solution.py:34
  44.6 2.0 broadcast_in_dim.39
  46.6 39.3 %scatter_fusion = f32[48,128,128]{2,1,0:T(8,128)} fusion(f32[48,128,128]{2,1,0:T(8,128)} %broadcast_in_dim.39, s32[192]{0:T(256)S(1)} %bitcast.45, f32[192,128,128]{2,1,0:T(8,128)} %copy.38), kind=kCustom, calls=%fused_computation.3 | custom fusion | flops 3145728 | bytes 37749504 | tf_op jit(solution)/shard_map/scatter-add | solution.py:35
  88.1 5.0 all-to-all-start
  93.1 3.1 slice.36
  96.5 4.2 all-to-all-done
  101.7 14.5 %all-to-all-start.1 = ((bf16[64,4,8,128]{3,2,1,0:T(8,128)(2,1)}), bf16[64,4,8,128]{3,2,1,0:T(8,128)(2,1)S(1)}, u32[]{:S(2)}, u32[]{:S(2)}) async-start(bf16[64,4,8,128]{3,2,1,0:T(8,128)(2,1)} %copy.41), calls=%async_computation.1 | async-start | bytes 1048576 | tf_op jit(solution)/shard_map/all_to_all | solution.py:43
  117.9 15.9 %all-to-all-done.1 = bf16[64,4,8,128]{3,2,1,0:T(8,128)(2,1)S(1)} async-done(((bf16[64,4,8,128]{3,2,1,0:T(8,128)(2,1)}), bf16[64,4,8,128]{3,2,1,0:T(8,128)(2,1)S(1)}, u32[]{:S(2)}, u32[]{:S(2)}) %all-to-all-start.1) | async-done | bytes 524320 | tf_op jit(solution)/shard_map/all_to_all | solution.py:43
  133.9 14.4 %scatter_custom_fusion.1 = f32[4096,128]{1,0:T(8,128)} fusion(f32[4096,128]{1,0:T(8,128)} %bitcast.40, s32[2048]{0:T(1024)S(1)} %bitcast.43, bf16[2048,128]{1,0:T(8,128)(2,1)S(1)} %bitcast.38, f32[]{:T(128)} %constant.8.clone.1, pred[2048]{0:T(1024)(128)(4,1)S(1)} %lt.56), kind=kCustom, calls=%fused_computation.26 | custom fusion | flops 786432 | bytes 2624000 | tf_op jit(solution)/shard_map/scatter-add | solution.py:55
  148.3 4.1 divide_convert_fusion
  152.4 8.0 %gather_fusion.1 = bf16[2048,128]{1,0:T(8,128)(2,1)} fusion(bf16[4096,128]{1,0:T(8,128)(2,1)S(1)} %get-tuple-element.20, s32[2048]{0:T(1024)S(1)} %broadcast_clamp_fusion), kind=kCustom, calls=%fused_computation.1 | custom fusion | bytes 1056768 | tf_op jit(solution)/shard_map/gather | solution.py:63
  161.8 11.6 %all_to_all.20 = bf16[64,4,8,128]{3,2,0,1:T(8,128)(2,1)S(1)} all-to-all(bf16[64,4,8,128]{3,2,0,1:T(8,128)(2,1)S(1)} %copy_select_fusion), channel_id=1, replica_groups=mesh['dom'=64,'local'=4] {'local'}, dimensions={1} | all-to-all | bytes 1048576 | tf_op jit(solution)/shard_map/all_to_all | solution.py:69
  174.3 6.4 %all-to-all-start.3 = ((bf16[64,4,8,128]{3,2,1,0:T(8,128)(2,1)}), bf16[64,4,8,128]{3,2,1,0:T(8,128)(2,1)}, u32[]{:S(2)}, u32[]{:S(2)}) async-start(bf16[64,4,8,128]{3,2,1,0:T(8,128)(2,1)} %copy.44), calls=%async_computation.3 | async-start | bytes 1048576 | tf_op jit(solution)/shard_map/all_to_all | solution.py:68
  180.7 3.9 fusion.18
  184.6 13.7 %all-to-all-done.3 = bf16[64,4,8,128]{3,2,1,0:T(8,128)(2,1)} async-done(((bf16[64,4,8,128]{3,2,1,0:T(8,128)(2,1)}), bf16[64,4,8,128]{3,2,1,0:T(8,128)(2,1)}, u32[]{:S(2)}, u32[]{:S(2)}) %all-to-all-start.3) | async-done | bytes 524320 | tf_op jit(solution)/shard_map/all_to_all | solution.py:68
  198.3 2.3 pad_maximum_fusion
  200.6 9.4 %gather_fusion.2 = bf16[192,128,128]{2,1,0:T(8,128)(2,1)} fusion(bf16[48,128,128]{2,1,0:T(8,128)(2,1)} %bitcast.35, s32[1024]{0:T(1024)S(1)} %pad_clamp_fusion), kind=kCustom, calls=%fused_computation.2 | custom fusion | bytes 12583680 | tf_op jit(solution)/shard_map/gather | solution.py:76
  210.0 11.4 %convolution_bitcast_fusion = f32[192,128,128]{1,2,0:T(8,128)} fusion(bf16[192,128,128]{2,1,0:T(8,128)(2,1)} %gather_fusion.2, bf16[192,128,128]{2,1,0:T(8,128)(2,1)} %param.14), kind=kOutput, calls=%fused_computation.11 | convolution fusion | flops 805306368 | bytes 25165824 | tf_op jit(solution)/shard_map/tij,tif->tjf/dot_general | solution.py:77
  221.3 12.6 %copy.46 = f32[192,128,128]{2,1,0:T(8,128)} copy(f32[192,128,128]{1,2,0:T(8,128)} %convolution_bitcast_fusion) | data formatting | bytes 25165824 | tf_op jit(solution)/shard_map/tij,tif->tjf/dot_general | solution.py:77
  235.5 38.7 %scatter_fusion.1 = f32[32,128,128]{2,1,0:T(8,128)} fusion(f32[32,128,128]{2,1,0:T(8,128)} %broadcast_in_dim.42, s32[192]{0:T(256)S(1)} %bitcast.44, f32[192,128,128]{2,1,0:T(8,128)} %copy.46), kind=kCustom, calls=%fused_computation.5 | custom fusion | flops 3145728 | bytes 37749504 | tf_op jit(solution)/shard_map/scatter-add | solution.py:80
  277.5 4.2 fusion
  281.7 239.3 %all-reduce.2.cloned.1.call-done = f32[256,256]{0,1:T(8,128)} async-done(((f32[256,256]{0,1:T(8,128)}), f32[256,256]{0,1:T(8,128)}) %all-reduce.2.cloned.1.call-update) | async-done | bytes 262160 | tf_op jit(solution)/shard_map/psum | solution.py:91
  (45 shorter events, 17.9 us)
Async XLA Ops:
  7.2 1.6 copy-start
  88.1 12.7 %all-to-all-start = ((bf16[64,4,8,128]{3,2,0,1:T(8,128)(2,1)}), bf16[64,4,8,128]{3,2,0,1:T(8,128)(2,1)S(1)}, u32[]{:S(2)}, u32[]{:S(2)}) async-start(bf16[64,4,8,128]{3,2,0,1:T(8,128)(2,1)} %copy.40), calls=%async_computation | async-start | bytes 1048576 | tf_op jit(solution)/shard_map/all_to_all | solution.py:44
  93.1 3.2 copy-start.5
  96.3 19.9 %copy-start.6 = (s32[1,256]{1,0:T(1,128)S(1)}, s32[1,256]{1,0:T(1,128)}, u32[]{:S(2)}) copy-start(s32[1,256]{1,0:T(1,128)} %param.17) | copy-start | bytes 3076
  96.3 20.1 %copy-start.4 = (s32[4096]{0:T(1024)S(1)}, s32[4096]{0:T(1024)}, u32[]{:S(2)}) copy-start(s32[4096]{0:T(1024)} %param.18) | copy-start | bytes 49156
  101.6 46.6 %copy-start.3 = (bf16[256,128]{1,0:T(8,128)(2,1)S(1)}, bf16[256,128]{1,0:T(8,128)(2,1)}, u32[]{:S(2)}) copy-start(bf16[256,128]{1,0:T(8,128)(2,1)} %param.11) | copy-start | bytes 196612
  101.7 46.6 %copy-start.7 = (f32[128]{0:T(128)S(1)}, f32[128]{0:T(128)}, u32[]{:S(2)}) copy-start(f32[128]{0:T(128)} %param.13) | copy-start | bytes 1540
  101.7 32.2 %all-to-all-start.1 = ((bf16[64,4,8,128]{3,2,1,0:T(8,128)(2,1)}), bf16[64,4,8,128]{3,2,1,0:T(8,128)(2,1)S(1)}, u32[]{:S(2)}, u32[]{:S(2)}) async-start(bf16[64,4,8,128]{3,2,1,0:T(8,128)(2,1)} %copy.41), calls=%async_computation.1 | async-start | bytes 1048576 | tf_op jit(solution)/shard_map/all_to_all | solution.py:43
  174.3 24.0 %all-to-all-start.3 = ((bf16[64,4,8,128]{3,2,1,0:T(8,128)(2,1)}), bf16[64,4,8,128]{3,2,1,0:T(8,128)(2,1)}, u32[]{:S(2)}, u32[]{:S(2)}) async-start(bf16[64,4,8,128]{3,2,1,0:T(8,128)(2,1)} %copy.44), calls=%async_computation.3 | async-start | bytes 1048576 | tf_op jit(solution)/shard_map/all_to_all | solution.py:68
  180.7 340.4 %all-reduce.2.cloned.1.call-start = ((), (), s32[]{:S(2)}) async-start(), calls=%async_computation.4 | async-start | bytes 524288 | tf_op jit(solution)/shard_map/psum | solution.py:91
  274.2 1.9 copy-start.1
  276.0 1.5 copy-start.2
Sparse Core Ops, SparseCore 0:
  277.6 243.3 all-reduce.1
where the time goes:
time: 533 us; the launch traced here: 530 us
  waiting for transfers between devices  273 us (51%)
  other arithmetic  99.6 us (19%)
  local copies, waits for them, and re-layouts  65.7 us (12%)
  matrix products  40.2 us (8%)
  starting transfers between devices  26 us (5%)
  between operations  14.2 us (3%)
  blocking collectives  11.6 us (2%)
    psum x1, waiting for transfers between devices, per_device(): summed = lax.psum(both_terms, ('dom', 'local'))  239 us
    scatter-add x1, other arithmetic, per_device(): jax.ops.segment_sum(products, dest_block, num_segments=dest_blocks)  39.3 us
    scatter-add x1, other arithmetic, per_device(): jax.ops.segment_sum(back_products, source_block, num_segments=source_blocks)  38.7 us
    all_to_all x1, waiting for transfers between devices, per_device(): lax.all_to_all(lax.all_to_all(outgoing, 'local', split_axis=1, concat_axi...  15.9 us
    all_to_all x1, starting transfers between devices, per_device(): lax.all_to_all(lax.all_to_all(outgoing, 'local', split_axis=1, concat_axi...  14.5 us
    scatter-add x1, other arithmetic, per_device(): partial_value[:root_rows].at[targets]  14.4 us
    all_to_all x1, waiting for transfers between devices, per_device(): lax.all_to_all(lax.all_to_all(returned, 'local', split_axis=1, concat_axi...  13.7 us
    dot_general x1, matrix products, per_device(): jnp.einsum('tij,tjf->tif', adjacency, picked, preferred_element_type=jnp....  13.6 us
  transfers between devices with their start and end apart: 4, of which 4 were waited for; matrix products, arithmetic and copies ran while one was open for 2% of the time, Pallas kernels for 0%

commit v1 on v0

v1 whole, which is shorter than its diff:
```python
import functools

import jax
import jax.numpy as jnp
from jax import lax
from jax.experimental import pallas as pl
from jax.experimental.pallas import tpu as pltpu
from jax.sharding import PartitionSpec as P

MESH = pl.DeviceIdType.MESH
F32 = jnp.float32
BF16 = jnp.bfloat16

NZ, NY, NX = 8, 4, 4
NXY = NY * NX
CAP = 8
BLOCK = 128
TILES = 192
OWN_BLOCKS = 32
CLONE_BLOCKS = 16
DEST_BLOCKS = OWN_BLOCKS + CLONE_BLOCKS
ROOTS = OWN_BLOCKS * BLOCK
MOST_OWN = TILES - CLONE_BLOCKS
MOST_CLONE = TILES - OWN_BLOCKS
PLANE = NXY * 2 * CAP
LOADS = 4

AT_FWD = 0
AT_BWD = AT_FWD + TILES
AT_LAST_FWD = AT_BWD + TILES
AT_LAST_BWD = AT_LAST_FWD + DEST_BLOCKS
TABLE = AT_LAST_BWD + 2 * OWN_BLOCKS


def step_offset(i):
    return 4 + (i // 2) * (1 - i % 2) - ((i + 1) // 2) * (i % 2)


def main_kernel(
    table, slot_s, features_h, weights, bias, adjacency_h, slot_v, degrees, cotangent,
    w_self, w_neigh,
    act_out, gfeat_out, gself_out, gneigh_out,
    feat, adj, proj, own, scan, scan_b, total, gmean, gpre, slots_t, gproj_t, rows_f,
    keep1, pass1, mate1, send1, mid1, land1,
    keep2, pass2, mate2, send2, mid2, land2,
    halves, mate_r, sum_r, z_r, sum_z, xy_r, done,
    load_sems, mate_send, mate_recv, xy_send, xy_recv, z_send, z_recv, own_sems,
    red_send, red_recv,
):
    dom = lax.axis_index("dom")
    x = lax.axis_index("local")
    core = dom % 2
    zy = dom // 2
    z = zy // NY
    y = zy % NY
    xy = y * NX + x
    mate = (dom + 1 - 2 * core, x)

    def xy_peer(k):
        py = (y + k // NX) % NY
        px = (x + k % NX) % NX
        return (z * NY + py) * 2 + core, px, py * NX + px

    def z_peer(dz):
        pz = (z + dz) % NZ
        return ((pz * NY + y) * 2 + core, x), pz

    barrier = pltpu.get_barrier_semaphore()
    pl.semaphore_signal(barrier, inc=1, device_id=mate, device_id_type=MESH)
    for k in range(1, NXY):
        pdom, px, _ = xy_peer(k)
        pl.semaphore_signal(barrier, inc=1, device_id=(pdom, px), device_id_type=MESH)
    for dz in range(1, NZ):
        pl.semaphore_signal(barrier, inc=1, device_id=z_peer(dz)[0], device_id_type=MESH)

    load_feat = pltpu.make_async_copy(features_h, feat, load_sems.at[LOADS])
    load_feat.start()
    share = TILES // LOADS
    load_adj = [
        pltpu.make_async_copy(
            adjacency_h.at[pl.ds(k * share, share)], adj.at[pl.ds(k * share, share)], load_sems.at[k]
        )
        for k in range(LOADS)
    ]
    for copy in load_adj:
        copy.start()

    load_feat.wait()
    rows = 512

    def project(i, carry):
        both = jnp.dot(feat[pl.ds(i * rows, rows), :], weights[...], preferred_element_type=F32)
        proj[pl.ds(i * (rows // BLOCK), rows // BLOCK)] = both[:, :BLOCK].astype(BF16).reshape(rows // BLOCK, BLOCK, BLOCK)
        own[pl.ds(i * (rows // BLOCK), rows // BLOCK)] = (both[:, BLOCK:] + bias[...]).reshape(rows // BLOCK, BLOCK, BLOCK)
        return carry

    lax.fori_loop(0, ROOTS // rows, project, 0, unroll=2)
    for copy in load_adj:
        copy.wait()

    def forward(i, acc):
        code = table[AT_FWD + i]
        tile = code & 255
        source = (code >> 8) & 255
        going = (code >> 24).astype(F32)
        acc = acc * going + jnp.dot(adj[tile], proj[source], preferred_element_type=F32)
        scan[i] = acc
        return acc

    lax.fori_loop(0, TILES, forward, jnp.zeros((BLOCK, BLOCK), F32), unroll=8)

    pl.semaphore_wait(barrier, 1 + (NXY - 1) + (NZ - 1))

    def start_swap(i, value, keep, away, back, lane):
        first = value[:, 0]
        second = value[:, 1]
        keep[i] = jnp.where(core == 0, first, second).reshape(NXY * CAP, BLOCK).astype(BF16)
        away[i] = jnp.where(core == 0, second, first).reshape(NXY * CAP, BLOCK).astype(BF16)
        swap(i, away, back, lane).start()

    def swap(i, away, back, lane):
        return pltpu.make_async_remote_copy(
            away.at[i], back.at[i], mate_send.at[lane, i], mate_recv.at[lane, i], device_id=mate, device_id_type=MESH
        )

    def start_xy(i, keep, away, back, send, mid, lane):
        swap(i, away, back, lane).wait()
        mine = keep[i].astype(F32).reshape(NXY, CAP, BLOCK)
        theirs = back[i].astype(F32).reshape(NXY, CAP, BLOCK)
        first = jnp.where(core == 0, mine, theirs)
        second = jnp.where(core == 0, theirs, mine)
        send[i] = jnp.concatenate([first, second], axis=1).astype(BF16)

        def go(k, carry):
            pdom, px, pxy = xy_peer(k)
            pltpu.make_async_remote_copy(
                send.at[i, pxy], mid.at[i, xy], xy_send.at[lane, i], xy_recv.at[lane, i],
                device_id=(pdom, px), device_id_type=MESH,
            ).start()
            return carry

        lax.fori_loop(1, NXY, go, 0)
        mid[i, xy] = send[i, xy]

    def wait_bytes(ref, sem):
        pltpu.make_async_copy(ref, ref, sem).wait()

    def z_copy(i, mid, land, lane):
        peer, _ = z_peer(step_offset(i))
        return pltpu.make_async_remote_copy(
            mid.at[i], land.at[z], z_send.at[lane, i], z_recv.at[lane, i], device_id=peer, device_id_type=MESH
        )

    def start_z(i, send, mid, land, lane):
        wait_bytes(mid.at[i, pl.ds(0, NXY - 1)], xy_recv.at[lane, i])
        wait_bytes(send.at[i, pl.ds(0, NXY - 1)], xy_send.at[lane, i])

        @pl.when(i < NZ - 1)
        def _():
            z_copy(i, mid, land, lane).start()

        @pl.when(i == NZ - 1)
        def _():
            pltpu.make_async_copy(mid.at[i], land.at[z], own_sems.at[lane]).start()

    def finish_z(i, mid, land, lane):
        @pl.when(i < NZ - 1)
        def _():
            z_copy(i, mid, land, lane).wait()

        @pl.when(i == NZ - 1)
        def _():
            pltpu.make_async_copy(mid.at[i], land.at[z], own_sems.at[lane]).wait()

        return (z + NZ - step_offset(i)) % NZ

    def send_partial(s, carry):
        @pl.when(s < NZ)
        def _():
            pz = (z + step_offset(s)) % NZ
            first = scan[table[AT_LAST_FWD + OWN_BLOCKS + 2 * pz]]
            second = scan[table[AT_LAST_FWD + OWN_BLOCKS + 2 * pz + 1]]
            value = jnp.concatenate([first, second], axis=0).reshape(NY, 2, NX, CAP, BLOCK)
            value = jnp.concatenate([value[:, 0].reshape(NXY, 1, CAP, BLOCK), value[:, 1].reshape(NXY, 1, CAP, BLOCK)], axis=1)
            start_swap(s, value, keep1, pass1, mate1, 0)

        @pl.when((s >= 1) & (s < NZ + 1))
        def _():
            start_xy(s - 1, keep1, pass1, mate1, send1, mid1, 0)

        @pl.when(s >= 3)
        def _():
            start_z(s - 3, send1, mid1, land1, 0)

        return carry

    lax.fori_loop(0, NZ + 3, send_partial, 0)

    def begin_total(b, carry):
        total[b] = scan[table[AT_LAST_FWD + b]]
        return carry

    lax.fori_loop(0, OWN_BLOCKS, begin_total, 0, unroll=4)

    def receive_plane(s, carry):
        plane = finish_z(s, mid1, land1, 0)
        arrived = land1[plane].reshape(PLANE, BLOCK)
        node = slot_v[pl.ds(plane, 1), :]
        row = lax.broadcasted_iota(jnp.int32, (BLOCK, PLANE), 0)

        def add(b, carry):
            hit = jnp.where(row == node - b * BLOCK, 1.0, 0.0).astype(BF16)
            total[b] += jnp.dot(hit, arrived, preferred_element_type=F32)
            return carry

        lax.fori_loop(0, OWN_BLOCKS, add, 0, unroll=4)
        return carry

    lax.fori_loop(0, NZ, receive_plane, 0)

    def activate(b, carry):
        degree = jnp.broadcast_to(degrees[pl.ds(b, 1), :].astype(F32), (BLOCK, BLOCK)).T
        scale = 1.0 / degree
        preact = own[b] + total[b] * scale
        sig = jax.nn.sigmoid(preact)
        act_out[b] = (preact * sig).astype(BF16)
        full = cotangent[b].astype(F32) * sig * (1.0 + preact * (1.0 - sig))
        gpre[b] = full.astype(BF16)
        mean = full * scale
        gmean[pl.ds(b * BLOCK, BLOCK), :] = mean
        slots_t[b] = mean.T.astype(BF16)
        return carry

    lax.fori_loop(0, OWN_BLOCKS, activate, 0, unroll=2)
    gmean[pl.ds(ROOTS, CAP), :] = jnp.zeros((CAP, BLOCK), F32)
    slots_t[DEST_BLOCKS] = jnp.zeros((BLOCK, BLOCK), BF16)
    scan[TILES] = jnp.zeros((BLOCK, BLOCK), F32)
    scan_b[MOST_CLONE] = jnp.zeros((BLOCK, BLOCK), F32)

    def back_own(i, acc):
        code = table[AT_BWD + i]
        tile = code & 255
        dest = (code >> 8) & 255
        going = (code >> 24).astype(F32)
        acc = acc * going + jnp.dot(slots_t[dest], adj[tile], preferred_element_type=F32)
        scan[i] = acc
        return acc

    per_step = MOST_OWN // NZ

    def send_back(s, acc):
        @pl.when(s < NZ)
        def _():
            pz = (z + step_offset(s)) % NZ

            def pick(q, carry):
                for j in range(CAP):
                    rows_f[pl.ds(q * CAP + j, 1), :] = gmean[pl.ds(slot_s[pz * PLANE + q * CAP + j], 1), :]
                return carry

            lax.fori_loop(0, 2 * NXY, pick, 0, unroll=4)
            start_swap(s, rows_f[...].reshape(NXY, 2, CAP, BLOCK), keep2, pass2, mate2, 1)

        @pl.when((s >= 1) & (s < NZ + 1))
        def _():
            start_xy(s - 1, keep2, pass2, mate2, send2, mid2, 1)

        @pl.when(s >= 3)
        def _():
            start_z(s - 3, send2, mid2, land2, 1)

        return acc

    def send_and_work(s, acc):
        send_back(s, 0)
        return lax.fori_loop(0, per_step, lambda i, a: back_own(s * per_step + i, a), acc, unroll=per_step // 2)

    acc = lax.fori_loop(0, NZ, send_and_work, jnp.zeros((BLOCK, BLOCK), F32))
    lax.fori_loop(NZ, NZ + 3, send_back, 0)

    def transposed_gpre(b, carry):
        at = pl.ds(pl.multiple_of(b * BLOCK, BLOCK), BLOCK)
        gproj_t[:, at] = gpre[b].astype(F32).T.astype(BF16)
        return carry

    lax.fori_loop(0, OWN_BLOCKS, transposed_gpre, 0, unroll=4)
    gself = jnp.dot(gproj_t[...], feat[...], preferred_element_type=F32).T

    def arrived_back(s, carry):
        plane = finish_z(s, mid2, land2, 1)
        value = land2[plane].astype(F32).reshape(NY, NX, 2, CAP, BLOCK)
        value = jnp.concatenate(
            [value[:, :, 0].reshape(NY, 1, NX, CAP, BLOCK), value[:, :, 1].reshape(NY, 1, NX, CAP, BLOCK)], axis=1
        ).reshape(2, BLOCK, BLOCK)
        slots_t[OWN_BLOCKS + 2 * plane] = value[0].T.astype(BF16)
        slots_t[OWN_BLOCKS + 2 * plane + 1] = value[1].T.astype(BF16)
        return carry

    lax.fori_loop(0, NZ, arrived_back, 0)

    def back_clone(i, acc):
        code = table[AT_BWD + OWN_BLOCKS + i]
        tile = code & 255
        dest = (code >> 16) & 255
        going = (code >> 24).astype(F32)
        acc = acc * going + jnp.dot(slots_t[dest], adj[tile], preferred_element_type=F32)
        scan_b[i] = acc
        return acc

    lax.fori_loop(0, MOST_CLONE, back_clone, jnp.zeros((BLOCK, BLOCK), F32), unroll=8)

    def gather_proj(c, carry):
        value = scan[table[AT_LAST_BWD + c]] + scan_b[table[AT_LAST_BWD + OWN_BLOCKS + c]]
        at = pl.ds(pl.multiple_of(c * BLOCK, BLOCK), BLOCK)
        gproj_t[:, at] = value.astype(BF16)
        return carry

    lax.fori_loop(0, OWN_BLOCKS, gather_proj, 0, unroll=4)
    gneigh = jnp.dot(gproj_t[...], feat[...], preferred_element_type=F32).T

    part = BLOCK // NZ
    halves[:, :, 0:part] = gself.reshape(2, NZ, part, BLOCK)
    halves[:, :, part:2 * part] = gneigh.reshape(2, NZ, part, BLOCK)
    copy = pltpu.make_async_remote_copy(
        halves.at[1 - core], mate_r, red_send.at[0], red_recv.at[0], device_id=mate, device_id_type=MESH
    )
    copy.start()
    copy.wait()
    sum_r[...] = halves[core] + mate_r[...]

    def along_z(src, dst, k):
        def go(dz, carry):
            peer, pz = z_peer(dz)
            pltpu.make_async_remote_copy(
                src(pz), dst, red_send.at[k], red_recv.at[k], device_id=peer, device_id_type=MESH
            ).start()
            return carry

        lax.fori_loop(1, NZ, go, 0)

    along_z(lambda pz: sum_r.at[pz], z_r.at[z], 1)
    z_r[z] = sum_r[z]
    wait_bytes(z_r.at[pl.ds(0, NZ - 1)], red_recv.at[1])
    wait_bytes(sum_r.at[pl.ds(0, NZ - 1)], red_send.at[1])
    value = z_r[0]
    for k in range(1, NZ):
        value = value + z_r[k]
    sum_z[...] = value

    def go_xy(k, carry):
        pdom, px, _ = xy_peer(k)
        pltpu.make_async_remote_copy(
            sum_z, xy_r.at[xy], red_send.at[2], red_recv.at[2], device_id=(pdom, px), device_id_type=MESH
        ).start()
        return carry

    lax.fori_loop(1, NXY, go_xy, 0)
    xy_r[xy] = sum_z[...]

    def give_features(c, carry):
        at = pl.ds(pl.multiple_of(c * BLOCK, BLOCK), BLOCK)
        value = lax.dot_general(gpre[c], w_self[...], (((1,), (1,)), ((), ())), preferred_element_type=F32)
        value += lax.dot_general(gproj_t[:, at], w_neigh[...], (((0,), (1,)), ((), ())), preferred_element_type=F32)
        gfeat_out[pl.ds(c * BLOCK, BLOCK), :] = value.astype(BF16)
        return carry

    lax.fori_loop(0, OWN_BLOCKS, give_features, 0, unroll=2)

    wait_bytes(xy_r.at[pl.ds(0, NXY - 1)], red_recv.at[2])
    wait_bytes(xy_r.at[pl.ds(0, NXY - 1)], red_send.at[2])
    value = xy_r[0]
    for k in range(1, NXY):
        value = value + xy_r[k]
    done[core, z] = value * (float(ROOTS * 2 * NZ * NXY) ** -0.5)

    along_z(lambda pz: done.at[core, z], done.at[core, z], 3)
    wait_bytes(done.at[core, pl.ds(0, NZ - 1)], red_recv.at[3])
    wait_bytes(done.at[core, pl.ds(0, NZ - 1)], red_send.at[3])
    copy = pltpu.make_async_remote_copy(
        done.at[core], done.at[core], red_send.at[4], red_recv.at[4], device_id=mate, device_id_type=MESH
    )
    copy.start()
    copy.wait()
    gself_out[...] = done[:, :, 0:part].reshape(2 * BLOCK, BLOCK)
    gneigh_out[...] = done[:, :, part:2 * part].reshape(2 * BLOCK, BLOCK)


def make_table(tile_at):
    dest = tile_at[:, 0]
    source = tile_at[:, 1]
    tile = jnp.arange(TILES, dtype=jnp.int32)
    is_clone = (dest >= OWN_BLOCKS).astype(jnp.int32)
    key = jnp.stack([dest, is_clone * OWN_BLOCKS + source])
    order = key * TILES + tile[None, :]
    rank = jnp.sum((order[:, None, :] < order[:, :, None]).astype(jnp.int32), axis=2)
    code = jnp.stack([
        tile | (source << 8),
        tile | (jnp.where(is_clone == 1, DEST_BLOCKS, dest) << 8) | (jnp.where(is_clone == 1, dest, DEST_BLOCKS) << 16),
    ])
    same = jnp.sum(((key[:, None, :] == key[:, :, None]) & (tile[None, None, :] < tile[None, :, None])).astype(jnp.int32), axis=2)
    code = code | ((same > 0).astype(jnp.int32) << 24)
    placed = jnp.sum(jnp.where(rank[:, None, :] == tile[None, :, None], code[:, None, :], 0), axis=2)
    block = jnp.arange(2 * OWN_BLOCKS, dtype=jnp.int32)
    upto = jnp.sum((key[:, None, :] <= block[None, :, None]).astype(jnp.int32), axis=2) - 1
    has = jnp.sum((key[1][None, :] == block[:, None]).astype(jnp.int32), axis=1) > 0
    last_own = jnp.where(has, upto[1], TILES)[:OWN_BLOCKS]
    last_clone = jnp.where(has, upto[1] - OWN_BLOCKS, MOST_CLONE)[OWN_BLOCKS:]
    return jnp.concatenate([placed[0], placed[1], upto[0, :DEST_BLOCKS], last_own, last_clone])


def per_device(
    features, w_self, w_neigh, bias_vector, adjacency, tile_at, clone_root, clone_count, degrees, cotangent
):
    table = make_table(tile_at)
    live = jnp.arange(CAP, dtype=jnp.int32)[None, :] < clone_count[0][:, None]
    slots = jnp.where(live, clone_root[0], ROOTS).reshape(NZ, NY, 2, NX, CAP)
    slots = slots.transpose(0, 1, 3, 2, 4).reshape(NZ, PLANE)
    weights = jnp.concatenate([w_neigh, w_self], axis=1)
    vmem = pl.BlockSpec(memory_space=pltpu.VMEM)
    smem = pl.BlockSpec(memory_space=pltpu.SMEM)
    hbm = pl.BlockSpec(memory_space=pl.ANY)
    V = pltpu.VMEM
    part = 2 * (BLOCK // NZ)
    exchange_bufs = [
        V((NZ, NXY * CAP, BLOCK), BF16),
        V((NZ, NXY * CAP, BLOCK), BF16),
        V((NZ, NXY * CAP, BLOCK), BF16),
        V((NZ, NXY, 2 * CAP, BLOCK), BF16),
        V((NZ, NXY, 2 * CAP, BLOCK), BF16),
        V((NZ, NXY, 2 * CAP, BLOCK), BF16),
    ]
    dma = pltpu.SemaphoreType.DMA
    act, gfeat, gself, gneigh = pl.pallas_call(
        main_kernel,
        out_shape=(
            jax.ShapeDtypeStruct((OWN_BLOCKS, BLOCK, BLOCK), BF16),
            jax.ShapeDtypeStruct((ROOTS, 2 * BLOCK), BF16),
            jax.ShapeDtypeStruct((2 * BLOCK, BLOCK), F32),
            jax.ShapeDtypeStruct((2 * BLOCK, BLOCK), F32),
        ),
        in_specs=[smem, smem, hbm, vmem, vmem, hbm, vmem, vmem, vmem, vmem, vmem],
        out_specs=(vmem, vmem, vmem, vmem),
        scratch_shapes=[
            V((ROOTS, 2 * BLOCK), BF16),
            V((TILES, BLOCK, BLOCK), BF16),
            V((OWN_BLOCKS, BLOCK, BLOCK), BF16),
            V((OWN_BLOCKS, BLOCK, BLOCK), F32),
            V((TILES + 1, BLOCK, BLOCK), F32),
            V((MOST_CLONE + 1, BLOCK, BLOCK), F32),
            V((OWN_BLOCKS, BLOCK, BLOCK), F32),
            V((ROOTS + CAP, BLOCK), F32),
            V((OWN_BLOCKS, BLOCK, BLOCK), BF16),
            V((DEST_BLOCKS + 1, BLOCK, BLOCK), BF16),
            V((BLOCK, ROOTS), BF16),
            V((PLANE, BLOCK), F32),
            *exchange_bufs,
            *exchange_bufs,
            V((2, NZ, part, BLOCK), F32),
            V((NZ, part, BLOCK), F32),
            V((NZ, part, BLOCK), F32),
            V((NZ, part, BLOCK), F32),
            V((part, BLOCK), F32),
            V((NXY, part, BLOCK), F32),
            V((2, NZ, part, BLOCK), F32),
            dma((LOADS + 1,)),
            dma((2, NZ)), dma((2, NZ)), dma((2, NZ)), dma((2, NZ)), dma((2, NZ)), dma((2, NZ)),
            dma((2,)),
            dma((5,)), dma((5,)),
        ],
        compiler_params=pltpu.CompilerParams(has_side_effects=True, collective_id=1, vmem_limit_bytes=60 << 20),
        name="layer",
    )(
        table, slots.reshape(-1), features, weights, bias_vector.reshape(1, BLOCK), adjacency, slots,
        degrees.reshape(OWN_BLOCKS, BLOCK), cotangent.reshape(OWN_BLOCKS, BLOCK, BLOCK), w_self, w_neigh,
    )
    return act.reshape(ROOTS, BLOCK), gfeat, gself, gneigh


def solution(mesh):
    split = ("dom", "local")
    placed = (
        P(split, None), P(), P(), P(), P(split, None, None), P(split, None), P(split, None, None),
        P(split, None), P(split), P(split, None),
    )
    return jax.shard_map(
        per_device,
        mesh=mesh,
        in_specs=placed,
        out_specs=(P(split, None), P(split, None), P(), P()),
        check_vma=False,
    )
```

time: 533 us -> 117 us (0.22)
  waiting for transfers between devices: 273 us -> 0 us
  Pallas kernels: 0 us -> 101 us
  other arithmetic: 99.6 us -> 5.36 us
  local copies, waits for them, and re-layouts: 65.7 us -> 8.92 us
  matrix products: 40.2 us -> 0 us
  starting transfers between devices: 26 us -> 0 us
  between operations: 14.2 us -> 0.73 us
  blocking collectives: 11.6 us -> 0 us
    psum x1 -> x0, waiting for transfers between devices: 239 us -> none  [per_device(): summed = lax.psum(both_terms, ('dom', 'local'))]
    pallas_call x0 -> x1, Pallas kernels: none -> 101 us  [per_device(): pl.pallas_call(main_kernel, out_shape=(jax.ShapeDtypeStruct((OWN_BLOCKS,...]
    scatter-add x3 -> x0, other arithmetic: 92.3 us -> none  [the longest x1 39.3 us: per_device(): jax.ops.segment_sum(products, dest_block, num_segments=dest_blocks)]
    dot_general x7 -> x0, matrix products: 40.2 us -> none  [the longest x1 13.6 us: per_device(): jnp.einsum('tij,tjf->tif', adjacency, picked, preferred_element_type=jnp....]
    all_to_all x3 -> x0, waiting for transfers between devices: 33.9 us -> none  [the longest x1 15.9 us: per_device(): lax.all_to_all(lax.all_to_all(outgoing, 'local', split_axis=1, concat_axi...]
    all_to_all x3 -> x0, starting transfers between devices: 25.9 us -> none  [the longest x1 14.5 us: per_device(): lax.all_to_all(lax.all_to_all(outgoing, 'local', split_axis=1, concat_axi...]
    gather x3 -> x0, local copies, waits for them, and re-layouts: 25.5 us -> none  [the longest x1 9.39 us: per_device(): dest_rows = slot_grad.reshape(dest_blocks, BLOCK, out_width)[dest_block]]
    dot_general x2 -> x0, local copies, waits for them, and re-layouts: 25.2 us -> none  [the longest x1 12.6 us: per_device(): jnp.einsum('tij,tif->tjf', adjacency, dest_rows, preferred_element_type=j...]
  transfers between devices with their start and end apart: 4 -> 0, of which waited for: 4 -> 0; matrix products, arithmetic and copies ran while one was open for 2% -> 0% of each run, Pallas kernels for 0% -> 0%
where the time goes in v1:
time: 117 us; the launch traced here: 116 us
  Pallas kernels  101 us (86%)
  local copies, waits for them, and re-layouts  8.92 us (8%)
  other arithmetic  5.36 us (5%)
    pallas_call x1, Pallas kernels, per_device(): pl.pallas_call(main_kernel, out_shape=(jax.ShapeDtypeStruct((OWN_BLOCKS,...  101 us
    unnamed x12, local copies, waits for them, and re-layouts  6.38 us

profile of v1, /device:TPU:1, one launch (start us, length us, event | category | flops | bytes accessed | tf_op | source)
XLA Modules:
  0.0 116.4 jit_solution(16229096827432386979)
XLA Ops:
  0.6 0.5 broadcast.179
  1.1 1.3 %reduce.3 = s32[256]{0:T(256)S(1)} reduce(s32[1,256]{1,0:T(1,128)} %param.17, s32[]{:T(128)} %broadcast.179), dimensions={0}, to_apply=%param.17.reduce_sub_computation.3 | reduce | bytes 2052 | tf_op args[7]
  2.5 0.8 fusion.7
  3.2 0.1 convert_reduce_fusion.3
  3.4 0.8 fusion.8
  4.1 0.1 convert_reduce_fusion.2
  4.3 0.1 slice.32
  4.4 0.1 lt.54
  4.5 0.4 convert_reduce_fusion
  4.9 0.2 select_reduce_fusion
  5.1 0.7 concatenate.18.table
  5.7 0.8 copy.21
  6.6 0.1 select_bitcast_fusion
  6.7 0.1 copy.22
  6.8 0.8 reshape.216.slot_v
  7.6 0.8 reshape_reshape.3.slot_s
  8.4 1.5 %pad_maximum_fusion.weights = bf16[256,256]{1,0:T(8,128)(2,1)} fusion(bf16[256,128]{1,0:T(8,128)(2,1)} %w_self.1, bf16[256,128]{1,0:T(8,128)(2,1)} %w_neigh.1), kind=kLoop, calls=%fused_computation.5 | loop fusion | flops 262144 | bytes 262144 | tf_op jit(solution)/shard_map/concatenate | solution.py:418
  9.9 101.3 %layer.1 = (bf16[32,128,128]{2,1,0:T(8,128)(2,1)}, bf16[4096,256]{1,0:T(8,128)(2,1)}, f32[256,128]{1,0:T(8,128)}, f32[256,128]{1,0:T(8,128)}) custom-call(s32[496]{0:T(512)} %concatenate.18.table, s32[2048]{0:T(1024)} %reshape_reshape.3.slot_s, bf16[4096,256]{1,0:T(8,128)(2,1)} %features_h.1, bf16[256,256]{1,0:T(8,128)(2,1)} %pad_maximum_fusion.weights, ...), custom_call_target="tpu_custom_call" | custom-call | tf_op jit(solution)/shard_map/layer/pallas_call | solution.py:433
  111.3 2.4 %copy.28 = bf16[4096,128]{1,0:T(8,128)(2,1)} copy(bf16[4096,128]{1,0:T(8,128)(2,1)} %bitcast.29) | data formatting | bytes 2097152
  113.7 0.0 copy-done
  113.7 1.3 %copy.29 = bf16[4096,256]{1,0:T(8,128)(2,1)} copy(bf16[4096,256]{1,0:T(8,128)(2,1)S(1)} %copy-done) | data formatting | bytes 4194304
  115.0 0.7 copy.30
  115.7 0.0 copy-done.1
  115.7 0.7 copy.31
  (11 shorter events, 0.1 us)
Async XLA Ops:
  111.3 2.4 %copy-start = (bf16[4096,256]{1,0:T(8,128)(2,1)S(1)}, bf16[4096,256]{1,0:T(8,128)(2,1)}, u32[]{:S(2)}) copy-start(bf16[4096,256]{1,0:T(8,128)(2,1)} %get-tuple-element.30) | copy-start | bytes 6291460
  113.7 1.3 %copy-start.2 = (f32[256,128]{1,0:T(8,128)S(1)}, f32[256,128]{1,0:T(8,128)}, u32[]{:S(2)}) copy-start(f32[256,128]{1,0:T(8,128)} %get-tuple-element.31) | copy-start | bytes 393220
  113.7 2.0 %copy-start.1 = (f32[256,128]{1,0:T(8,128)S(1)}, f32[256,128]{1,0:T(8,128)}, u32[]{:S(2)}) copy-start(f32[256,128]{1,0:T(8,128)} %get-tuple-element.32) | copy-start | bytes 393220

commit v2 on v1

v2 whole, which is shorter than its diff:
```python
import functools

import jax
import jax.numpy as jnp
from jax import lax
from jax.experimental import pallas as pl
from jax.experimental.pallas import tpu as pltpu
from jax.sharding import PartitionSpec as P

MESH = pl.DeviceIdType.MESH
F32 = jnp.float32
BF16 = jnp.bfloat16

NZ, NY, NX = 8, 4, 4
NXY = NY * NX
CAP = 8
BLOCK = 128
TILES = 192
OWN_BLOCKS = 32
CLONE_BLOCKS = 16
DEST_BLOCKS = OWN_BLOCKS + CLONE_BLOCKS
ROOTS = OWN_BLOCKS * BLOCK
MOST_OWN = TILES - CLONE_BLOCKS
MOST_CLONE = TILES - OWN_BLOCKS
PLANE = NXY * 2 * CAP
LOADS = 4

FWD, BWD, LAST_FWD, LAST_BWD = 0, 1, 2, 3
PART = 2 * BLOCK // NXY


def step_offset(i):
    return 4 + (i // 2) * (1 - i % 2) - ((i + 1) // 2) * (i % 2)


def make_table(tiles_at, out):
    across = lax.broadcasted_iota(jnp.int32, (TILES, TILES), 1)
    down = lax.broadcasted_iota(jnp.int32, (TILES, TILES), 0)

    def column(row):
        return jnp.sum(jnp.where(across == down, row, 0), axis=1, keepdims=True)

    dest = tiles_at[0:1, :]
    source = tiles_at[1:2, :]
    dest_c = column(dest)
    source_c = column(source)
    tile_c = lax.broadcasted_iota(jnp.int32, (TILES, 1), 0)
    tile = lax.broadcasted_iota(jnp.int32, (1, TILES), 1)
    is_clone = dest_c >= OWN_BLOCKS
    block = lax.broadcasted_iota(jnp.int32, (TILES, BLOCK), 1)
    key_b = source + jnp.where(dest >= OWN_BLOCKS, OWN_BLOCKS, 0)
    key_b_c = source_c + jnp.where(is_clone, OWN_BLOCKS, 0)
    code_f = tile_c + source_c * 256
    code_b = tile_c + jnp.where(is_clone, DEST_BLOCKS, dest_c) * 256 + jnp.where(is_clone, dest_c, DEST_BLOCKS) * 65536
    for at, last, key, key_c, code in ((FWD, LAST_FWD, dest, dest_c, code_f), (BWD, LAST_BWD, key_b, key_b_c, code_b)):
        before = (key * TILES + tile) < (key_c * TILES + tile_c)
        rank = jnp.sum(jnp.where(before, 1, 0), axis=1, keepdims=True)
        same = jnp.sum(jnp.where(before & (key == key_c), 1, 0), axis=1, keepdims=True)
        code = code + jnp.where(same > 0, 1 << 24, 0)
        out[at:at + 1, 0:TILES] = jnp.sum(jnp.where(rank == across, code, 0), axis=0, keepdims=True)
        upto = jnp.sum(jnp.where(key_c <= block, 1, 0), axis=0, keepdims=True) - 1
        if at == BWD:
            has = jnp.sum(jnp.where(key_c == block, 1, 0), axis=0, keepdims=True) > 0
            lane = lax.broadcasted_iota(jnp.int32, (1, BLOCK), 1)
            own = jnp.where(has, upto, TILES)
            clone = jnp.where(has, upto - OWN_BLOCKS, TILES)
            upto = jnp.where(lane < OWN_BLOCKS, own, clone)
        out[last:last + 1, 0:BLOCK] = upto


def main_kernel(
    tiles_at, root_t, count, features_h, adjacency_h, cotangent_h, bias, degrees, w_self, w_neigh,
    act_out, gfeat_out, gself_out, gneigh_out,
    table_v, table, slot_n, slot_s, slot_v, weights, cotangent, act, gfeat,
    feat, adj, proj, own, scan, total, scale, gmean, gpre, slots_t, gproj_t, rows_f,
    keep1, pass1, mate1, send1, mid1, land1,
    keep2, pass2, mate2, send2, mid2, land2,
    pieces, xy_r, sum_xy, z_r, sum_z, mate_r, done,
    load_sems, mate_send, mate_recv, xy_send, xy_recv, z_send, z_recv, own_sems,
    red_send, red_recv, out_sems,
):
    dom = lax.axis_index("dom")
    x = lax.axis_index("local")
    core = dom % 2
    zy = dom // 2
    z = zy // NY
    y = zy % NY
    xy = y * NX + x
    mate = (dom + 1 - 2 * core, x)

    def xy_peer(k):
        py = (y + k // NX) % NY
        px = (x + k % NX) % NX
        return (z * NY + py) * 2 + core, px, py * NX + px

    def z_peer(dz):
        pz = (z + dz) % NZ
        return ((pz * NY + y) * 2 + core, x), pz

    barrier = pltpu.get_barrier_semaphore()
    pl.semaphore_signal(barrier, inc=1, device_id=mate, device_id_type=MESH)
    for k in range(1, NXY):
        pdom, px, _ = xy_peer(k)
        pl.semaphore_signal(barrier, inc=1, device_id=(pdom, px), device_id_type=MESH)
    for dz in range(1, NZ):
        pl.semaphore_signal(barrier, inc=1, device_id=z_peer(dz)[0], device_id_type=MESH)

    load_feat = pltpu.make_async_copy(features_h, feat, load_sems.at[LOADS])
    load_feat.start()
    share = TILES // LOADS
    load_adj = [
        pltpu.make_async_copy(
            adjacency_h.at[pl.ds(k * share, share)], adj.at[pl.ds(k * share, share)], load_sems.at[k]
        )
        for k in range(LOADS)
    ]
    for copy in load_adj:
        copy.start()
    load_cot = pltpu.make_async_copy(cotangent_h, cotangent, load_sems.at[LOADS + 1])
    load_cot.start()

    make_table(tiles_at[...], table_v)
    live = lax.broadcasted_iota(jnp.int32, (CAP, 2 * NZ * NXY), 0) < count[...]
    slot_n[...] = jnp.where(live, root_t[...], ROOTS)
    table_copy = pltpu.make_async_copy(table_v, table, load_sems.at[LOADS + 2])
    slot_copy = pltpu.make_async_copy(slot_n, slot_s, load_sems.at[LOADS + 3])
    table_copy.start()
    slot_copy.start()

    weights[:, 0:BLOCK] = w_neigh[...]
    weights[:, BLOCK:2 * BLOCK] = w_self[...]

    load_feat.wait()
    rows = 512

    def project(i, carry):
        both = jnp.dot(feat[pl.ds(i * rows, rows), :], weights[...], preferred_element_type=F32)
        proj[pl.ds(i * (rows // BLOCK), rows // BLOCK)] = both[:, :BLOCK].astype(BF16).reshape(rows // BLOCK, BLOCK, BLOCK)
        own[pl.ds(i * (rows // BLOCK), rows // BLOCK)] = (both[:, BLOCK:] + bias[...]).reshape(rows // BLOCK, BLOCK, BLOCK)
        return carry

    lax.fori_loop(0, ROOTS // rows, project, 0, unroll=4)
    for copy in load_adj:
        copy.wait()
    table_copy.wait()
    slot_copy.wait()

    def forward(i, acc):
        code = table[FWD, i]
        tile = code & 255
        source = (code >> 8) & 255
        going = (code >> 24).astype(F32)
        acc = acc * going + jnp.dot(adj[tile], proj[source], preferred_element_type=F32)
        scan[i] = acc
        return acc

    lax.fori_loop(0, TILES, forward, jnp.zeros((BLOCK, BLOCK), F32), unroll=24)

    pl.semaphore_wait(barrier, 1 + (NXY - 1) + (NZ - 1))

    def start_swap(i, value, keep, away, back, lane):
        first = value[:, 0]
        second = value[:, 1]
        keep[i] = jnp.where(core == 0, first, second).reshape(NXY * CAP, BLOCK).astype(BF16)
        away[i] = jnp.where(core == 0, second, first).reshape(NXY * CAP, BLOCK).astype(BF16)
        swap(i, away, back, lane).start()

    def swap(i, away, back, lane):
        return pltpu.make_async_remote_copy(
            away.at[i], back.at[i], mate_send.at[lane, i], mate_recv.at[lane, i], device_id=mate, device_id_type=MESH
        )

    def start_xy(i, keep, away, back, send, mid, lane):
        swap(i, away, back, lane).wait()
        mine = keep[i].astype(F32).reshape(NXY, CAP, BLOCK)
        theirs = back[i].astype(F32).reshape(NXY, CAP, BLOCK)
        first = jnp.where(core == 0, mine, theirs)
        second = jnp.where(core == 0, theirs, mine)
        send[i] = jnp.concatenate([first, second], axis=1).astype(BF16)

        def go(k, carry):
            pdom, px, pxy = xy_peer(k)
            pltpu.make_async_remote_copy(
                send.at[i, pxy], mid.at[i, xy], xy_send.at[lane, i], xy_recv.at[lane, i],
                device_id=(pdom, px), device_id_type=MESH,
            ).start()
            return carry

        lax.fori_loop(1, NXY, go, 0)
        mid[i, xy] = send[i, xy]

    def wait_bytes(ref, sem):
        pltpu.make_async_copy(ref, ref, sem).wait()

    def z_copy(i, mid, land, lane):
        peer, _ = z_peer(step_offset(i))
        return pltpu.make_async_remote_copy(
            mid.at[i], land.at[z], z_send.at[lane, i], z_recv.at[lane, i], device_id=peer, device_id_type=MESH
        )

    def start_z(i, send, mid, land, lane):
        wait_bytes(mid.at[i, pl.ds(0, NXY - 1)], xy_recv.at[lane, i])
        wait_bytes(send.at[i, pl.ds(0, NXY - 1)], xy_send.at[lane, i])

        @pl.when(i < NZ - 1)
        def _():
            z_copy(i, mid, land, lane).start()

        @pl.when(i == NZ - 1)
        def _():
            pltpu.make_async_copy(mid.at[i], land.at[z], own_sems.at[lane]).start()

    def finish_z(i, mid, land, lane):
        @pl.when(i < NZ - 1)
        def _():
            z_copy(i, mid, land, lane).wait()

        @pl.when(i == NZ - 1)
        def _():
            pltpu.make_async_copy(mid.at[i], land.at[z], own_sems.at[lane]).wait()

        return (z + NZ - step_offset(i)) % NZ

    def send_partial(s, carry):
        pz = (z + step_offset(s)) % NZ
        first = scan[table[LAST_FWD, OWN_BLOCKS + 2 * pz]]
        second = scan[table[LAST_FWD, OWN_BLOCKS + 2 * pz + 1]]
        value = jnp.concatenate([first, second], axis=0).reshape(NY, 2, NX, CAP, BLOCK)
        value = jnp.concatenate([value[:, 0].reshape(NXY, 1, CAP, BLOCK), value[:, 1].reshape(NXY, 1, CAP, BLOCK)], axis=1)
        start_swap(s, value, keep1, pass1, mate1, 0)
        return carry

    lax.fori_loop(0, NZ, send_partial, 0)

    def send_xy(s, carry):
        start_xy(s, keep1, pass1, mate1, send1, mid1, 0)
        return carry

    lax.fori_loop(0, NZ, send_xy, 0)

    def send_z(s, carry):
        start_z(s, send1, mid1, land1, 0)
        return carry

    lax.fori_loop(0, NZ, send_z, 0)

    node = slot_n[...].astype(F32)
    high = jnp.floor(node * (1.0 / 64.0))
    low = node - high * 64.0
    both = jnp.concatenate([high, low], axis=0).astype(BF16)
    lane = lax.broadcasted_iota(jnp.int32, (2 * NZ * NXY, PLANE), 1)
    device = (lane // 64) * 8 + ((lane // 8) % 2) * 4 + (lane // 16) % 4
    down = lax.broadcasted_iota(jnp.int32, (2 * NZ * NXY, PLANE), 0)
    lane_cap = lax.broadcasted_iota(jnp.int32, (CAP, PLANE), 1) % CAP
    down_cap = lax.broadcasted_iota(jnp.int32, (CAP, PLANE), 0)
    for p in range(NZ):
        pick = jnp.where(down == device + p * 2 * NXY, 1.0, 0.0).astype(BF16)
        value = jnp.dot(both, pick, preferred_element_type=F32)
        value = value[0:CAP] * 64.0 + value[CAP:2 * CAP]
        slot_v[p:p + 1, :] = jnp.sum(jnp.where(lane_cap == down_cap, value, 0.0), axis=0, keepdims=True).astype(jnp.int32)
    def begin_total(b, carry):
        total[b] = scan[table[LAST_FWD, b]]
        inverse = 1.0 / degrees[pl.ds(b, 1), :].astype(F32)
        scale[b] = jnp.broadcast_to(inverse, (BLOCK, BLOCK)).T
        return carry

    lax.fori_loop(0, OWN_BLOCKS, begin_total, 0, unroll=2)

    def receive_plane(s, carry):
        plane = finish_z((s + NZ - 1) % NZ, mid1, land1, 0)
        arrived = land1[plane].reshape(PLANE, BLOCK)
        node = slot_v[pl.ds(plane, 1), :]
        row = lax.broadcasted_iota(jnp.int32, (BLOCK, PLANE), 0)

        def add(b, carry):
            hit = jnp.where(row == node - b * BLOCK, 1.0, 0.0).astype(BF16)
            total[b] += jnp.dot(hit, arrived, preferred_element_type=F32)
            return carry

        lax.fori_loop(0, OWN_BLOCKS, add, 0, unroll=OWN_BLOCKS)
        return carry

    lax.fori_loop(0, NZ, receive_plane, 0)
    load_cot.wait()

    def activate(b, carry):
        preact = own[b] + total[b] * scale[b]
        sig = jax.nn.sigmoid(preact)
        act[b] = (preact * sig).astype(BF16)
        full = cotangent[b].astype(F32) * sig * (1.0 + preact * (1.0 - sig))
        gpre[b] = full.astype(BF16)
        gmean[pl.ds(b * BLOCK, BLOCK), :] = full * scale[b]
        return carry

    lax.fori_loop(0, OWN_BLOCKS, activate, 0, unroll=2)
    give_act = pltpu.make_async_copy(act, act_out, out_sems.at[0])
    give_act.start()
    gmean[pl.ds(ROOTS, CAP), :] = jnp.zeros((CAP, BLOCK), F32)
    slots_t[DEST_BLOCKS] = jnp.zeros((BLOCK, BLOCK), BF16)
    scan[TILES] = jnp.zeros((BLOCK, BLOCK), F32)

    def back_own(i, acc):
        code = table[BWD, i]
        tile = code & 255
        dest = (code >> 8) & 255
        going = (code >> 24).astype(F32)
        acc = acc * going + jnp.dot(slots_t[dest], adj[tile], preferred_element_type=F32)
        scan[i] = acc
        return acc

    def gather_plane(s, carry):
        pz = (z + step_offset(s)) % NZ

        def pick(q, carry):
            d = pz * 2 * NXY + (q // 8) * 8 + (q % 2) * 4 + (q // 2) % 4
            for j in range(CAP):
                rows_f[pl.ds(q * CAP + j, 1), :] = gmean[pl.ds(slot_s[j, d], 1), :]
            return carry

        lax.fori_loop(0, 2 * NXY, pick, 0, unroll=16)
        start_swap(s, rows_f[...].reshape(NXY, 2, CAP, BLOCK), keep2, pass2, mate2, 1)
        return carry

    def send_back(s, carry):
        gather_plane(s, 0)

        @pl.when(s >= 2)
        def _():
            start_xy(s - 2, keep2, pass2, mate2, send2, mid2, 1)

        @pl.when(s >= 5)
        def _():
            start_z(s - 5, send2, mid2, land2, 1)

        return carry

    lax.fori_loop(0, NZ, send_back, 0)
    start_xy(NZ - 2, keep2, pass2, mate2, send2, mid2, 1)

    def transpose(b, carry):
        at = pl.ds(pl.multiple_of(b * BLOCK, BLOCK), BLOCK)
        gproj_t[:, at] = gpre[b].astype(F32).T.astype(BF16)
        slots_t[b] = gmean[pl.ds(b * BLOCK, BLOCK), :].T.astype(BF16)
        return carry

    lax.fori_loop(0, OWN_BLOCKS // 2, transpose, 0, unroll=2)
    start_xy(NZ - 1, keep2, pass2, mate2, send2, mid2, 1)
    start_z(NZ - 5, send2, mid2, land2, 1)
    start_z(NZ - 4, send2, mid2, land2, 1)
    lax.fori_loop(OWN_BLOCKS // 2, OWN_BLOCKS, transpose, 0, unroll=2)
    start_z(NZ - 3, send2, mid2, land2, 1)
    start_z(NZ - 2, send2, mid2, land2, 1)
    start_z(NZ - 1, send2, mid2, land2, 1)
    gself = jnp.dot(gproj_t[...], feat[...], preferred_element_type=F32).T

    def wait_both(ref, lane, k):
        wait_bytes(ref, red_recv.at[lane, k])
        wait_bytes(ref, red_send.at[lane, k])

    def around_xy(src, dst, lane, k):
        def go(j, carry):
            pdom, px, pxy = xy_peer(j)
            pltpu.make_async_remote_copy(
                src(pxy), dst, red_send.at[lane, k], red_recv.at[lane, k],
                device_id=(pdom, px), device_id_type=MESH,
            ).start()
            return carry

        lax.fori_loop(1, NXY, go, 0)

    def swap_sums(lane):
        return pltpu.make_async_remote_copy(
            sum_z.at[lane], mate_r.at[lane], red_send.at[lane, 2], red_recv.at[lane, 2],
            device_id=mate, device_id_type=MESH,
        )

    def reduce_0(value, lane):
        pieces[lane] = value.reshape(NXY, PART, BLOCK)
        around_xy(lambda pxy: pieces.at[lane, pxy], xy_r.at[lane, xy], lane, 0)
        xy_r[lane, xy] = pieces[lane, xy]

    def reduce_1(lane):
        wait_both(xy_r.at[lane, pl.ds(0, NXY - 1)], lane, 0)
        value = xy_r[lane, 0]
        for k in range(1, NXY):
            value = value + xy_r[lane, k]
        sum_xy[lane] = value

        def go(dz, carry):
            peer, _ = z_peer(dz)
            pltpu.make_async_remote_copy(
                sum_xy.at[lane], z_r.at[lane, z], red_send.at[lane, 1], red_recv.at[lane, 1],
                device_id=peer, device_id_type=MESH,
            ).start()
            return carry

        lax.fori_loop(1, NZ, go, 0)
        z_r[lane, z] = value

    def reduce_2(lane):
        wait_both(z_r.at[lane, pl.ds(0, NZ - 1)], lane, 1)
        value = z_r[lane, 0]
        for k in range(1, NZ):
            value = value + z_r[lane, k]
        sum_z[lane] = value
        swap_sums(lane).start()

    def reduce_3(lane):
        swap_sums(lane).wait()
        done[lane, xy] = (sum_z[lane] + mate_r[lane]) * (float(ROOTS * 2 * NZ * NXY) ** -0.5)
        around_xy(lambda pxy: done.at[lane, xy], done.at[lane, xy], lane, 3)

    def reduce_4(lane, out):
        wait_both(done.at[lane, pl.ds(0, NXY - 1)], lane, 3)
        out[...] = done[lane].reshape(2 * BLOCK, BLOCK)

    reduce_0(gself, 0)
    lax.fori_loop(0, MOST_OWN, back_own, jnp.zeros((BLOCK, BLOCK), F32), unroll=22)

    def keep_own(c, carry):
        total[c] = scan[table[LAST_BWD, c]]
        return carry

    lax.fori_loop(0, OWN_BLOCKS, keep_own, 0, unroll=4)

    def arrived_back(s, carry):
        plane = finish_z((s + NZ - 1) % NZ, mid2, land2, 1)
        value = land2[plane].astype(F32).reshape(NY, NX, 2, CAP, BLOCK)
        value = jnp.concatenate(
            [value[:, :, 0].reshape(NY, 1, NX, CAP, BLOCK), value[:, :, 1].reshape(NY, 1, NX, CAP, BLOCK)], axis=1
        ).reshape(2, BLOCK, BLOCK)
        slots_t[OWN_BLOCKS + 2 * plane] = value[0].T.astype(BF16)
        slots_t[OWN_BLOCKS + 2 * plane + 1] = value[1].T.astype(BF16)
        return carry

    lax.fori_loop(0, NZ, arrived_back, 0)
    reduce_1(0)

    def back_clone(i, acc):
        code = table[BWD, OWN_BLOCKS + i]
        tile = code & 255
        dest = (code >> 16) & 255
        going = (code >> 24).astype(F32)
        acc = acc * going + jnp.dot(slots_t[dest], adj[tile], preferred_element_type=F32)
        scan[i] = acc
        return acc

    lax.fori_loop(0, MOST_CLONE, back_clone, jnp.zeros((BLOCK, BLOCK), F32), unroll=20)

    def gather_proj(c, carry):
        value = total[c] + scan[table[LAST_BWD, OWN_BLOCKS + c]]
        at = pl.ds(pl.multiple_of(c * BLOCK, BLOCK), BLOCK)
        gproj_t[:, at] = value.astype(BF16)
        return carry

    lax.fori_loop(0, OWN_BLOCKS, gather_proj, 0, unroll=4)
    reduce_2(0)
    gneigh = jnp.dot(gproj_t[...], feat[...], preferred_element_type=F32).T

    reduce_0(gneigh, 1)
    reduce_3(0)

    def give_features(c, carry):
        at = pl.ds(pl.multiple_of(c * BLOCK, BLOCK), BLOCK)
        value = lax.dot_general(gpre[c], w_self[...], (((1,), (1,)), ((), ())), preferred_element_type=F32)
        value += lax.dot_general(gproj_t[:, at], w_neigh[...], (((0,), (1,)), ((), ())), preferred_element_type=F32)
        gfeat[pl.ds(c * BLOCK, BLOCK), :] = value.astype(BF16)
        return carry

    lax.fori_loop(0, OWN_BLOCKS // 4, give_features, 0, unroll=8)
    reduce_1(1)
    lax.fori_loop(OWN_BLOCKS // 4, OWN_BLOCKS // 2, give_features, 0, unroll=8)
    reduce_2(1)
    lax.fori_loop(OWN_BLOCKS // 2, OWN_BLOCKS // 4 * 3, give_features, 0, unroll=8)
    reduce_3(1)
    lax.fori_loop(OWN_BLOCKS // 4 * 3, OWN_BLOCKS, give_features, 0, unroll=8)
    give_feat = pltpu.make_async_copy(gfeat, gfeat_out, out_sems.at[1])
    give_feat.start()
    reduce_4(0, gself_out)
    reduce_4(1, gneigh_out)
    give_act.wait()
    give_feat.wait()


def finish_kernel(act, gfeat, gself, gneigh, act_out, gfeat_out, gself_out, gneigh_out, sems):
    copies = [
        pltpu.make_async_copy(src, dst, sems.at[k])
        for k, (src, dst) in enumerate(
            ((gfeat, gfeat_out), (act, act_out), (gself, gself_out), (gneigh, gneigh_out))
        )
    ]
    for copy in copies:
        copy.start()
    for copy in copies:
        copy.wait()


def per_device(
    features, w_self, w_neigh, bias_vector, adjacency, tile_at, clone_root, clone_count, degrees, cotangent
):
    vmem = pl.BlockSpec(memory_space=pltpu.VMEM)
    hbm = pl.BlockSpec(memory_space=pl.ANY)
    V = pltpu.VMEM
    exchange_bufs = [
        V((NZ, NXY * CAP, BLOCK), BF16),
        V((NZ, NXY * CAP, BLOCK), BF16),
        V((NZ, NXY * CAP, BLOCK), BF16),
        V((NZ, NXY, 2 * CAP, BLOCK), BF16),
        V((NZ, NXY, 2 * CAP, BLOCK), BF16),
        V((NZ, NXY, 2 * CAP, BLOCK), BF16),
    ]
    dma = pltpu.SemaphoreType.DMA
    outs = (
        jax.ShapeDtypeStruct((OWN_BLOCKS, BLOCK, BLOCK), BF16),
        jax.ShapeDtypeStruct((ROOTS, 2 * BLOCK), BF16),
        jax.ShapeDtypeStruct((2 * BLOCK, BLOCK), F32),
        jax.ShapeDtypeStruct((2 * BLOCK, BLOCK), F32),
    )
    results = pl.pallas_call(
        main_kernel,
        out_shape=outs,
        in_specs=[vmem, vmem, vmem, hbm, hbm, hbm, vmem, vmem, vmem, vmem],
        out_specs=(hbm, hbm, vmem, vmem),
        scratch_shapes=[
            V((8, 256), jnp.int32),
            pltpu.SMEM((8, 256), jnp.int32),
            V((CAP, 2 * NZ * NXY), jnp.int32),
            pltpu.SMEM((CAP, 2 * NZ * NXY), jnp.int32),
            V((NZ, PLANE), jnp.int32),
            V((2 * BLOCK, 2 * BLOCK), BF16),
            V((OWN_BLOCKS, BLOCK, BLOCK), BF16),
            V((OWN_BLOCKS, BLOCK, BLOCK), BF16),
            V((ROOTS, 2 * BLOCK), BF16),
            V((ROOTS, 2 * BLOCK), BF16),
            V((TILES, BLOCK, BLOCK), BF16),
            V((OWN_BLOCKS, BLOCK, BLOCK), BF16),
            V((OWN_BLOCKS, BLOCK, BLOCK), F32),
            V((TILES + 1, BLOCK, BLOCK), F32),
            V((OWN_BLOCKS, BLOCK, BLOCK), F32),
            V((OWN_BLOCKS, BLOCK, BLOCK), F32),
            V((ROOTS + CAP, BLOCK), F32),
            V((OWN_BLOCKS, BLOCK, BLOCK), BF16),
            V((DEST_BLOCKS + 1, BLOCK, BLOCK), BF16),
            V((BLOCK, ROOTS), BF16),
            V((PLANE, BLOCK), F32),
            *exchange_bufs,
            *exchange_bufs,
            V((2, NXY, PART, BLOCK), F32),
            V((2, NXY, PART, BLOCK), F32),
            V((2, PART, BLOCK), F32),
            V((2, NZ, PART, BLOCK), F32),
            V((2, PART, BLOCK), F32),
            V((2, PART, BLOCK), F32),
            V((2, NXY, PART, BLOCK), F32),
            dma((LOADS + 4,)),
            dma((2, NZ)), dma((2, NZ)), dma((2, NZ)), dma((2, NZ)), dma((2, NZ)), dma((2, NZ)),
            dma((2,)),
            dma((2, 4)), dma((2, 4)), dma((2,)),
        ],
        compiler_params=pltpu.CompilerParams(has_side_effects=True, collective_id=1, vmem_limit_bytes=60 << 20),
        name="layer",
    )(
        tile_at.T, clone_root[0].T, clone_count, features, adjacency, cotangent.reshape(OWN_BLOCKS, BLOCK, BLOCK),
        bias_vector.reshape(1, BLOCK), degrees.reshape(OWN_BLOCKS, BLOCK), w_self, w_neigh,
    )
    act, gfeat, gself, gneigh = pl.pallas_call(
        finish_kernel,
        out_shape=outs,
        in_specs=[vmem] * 4,
        out_specs=(hbm,) * 4,
        scratch_shapes=[dma((4,))],
        name="finish",
    )(*results)
    return act.reshape(ROOTS, BLOCK), gfeat, gself, gneigh


def solution(mesh):
    split = ("dom", "local")
    placed = (
        P(split, None), P(), P(), P(), P(split, None, None), P(split, None), P(split, None, None),
        P(split, None), P(split), P(split, None),
    )
    return jax.shard_map(
        per_device,
        mesh=mesh,
        in_specs=placed,
        out_specs=(P(split, None), P(split, None), P(), P()),
        check_vma=False,
    )
```

time: 117 us -> 86.5 us (0.74)
  Pallas kernels: 101 us -> 85.8 us
  local copies, waits for them, and re-layouts: 8.92 us -> 0 us
  other arithmetic: 5.36 us -> 0 us
    pallas_call x1 -> x2, Pallas kernels: 101 us -> 85.8 us  [the longest x1 82.1 us: per_device(): pl.pallas_call(main_kernel, out_shape=outs, in_specs=[vmem, vmem, vmem, h...]
    unnamed x12 -> x0, local copies, waits for them, and re-layouts: 6.38 us -> none
    concatenate x1 -> x0, other arithmetic: 1.54 us -> none  [per_device(): weights = jnp.concatenate([w_neigh, w_self], axis=1)]
    unnamed x1 -> x0, other arithmetic: 1.34 us -> none
where the time goes in v2:
time: 86.5 us; the launch traced here: 86.4 us
  Pallas kernels  85.8 us (99%)
    pallas_call x1, Pallas kernels, per_device(): pl.pallas_call(main_kernel, out_shape=outs, in_specs=[vmem, vmem, vmem, h...  82.1 us
    pallas_call x1, Pallas kernels, per_device(): pl.pallas_call(finish_kernel, out_shape=outs, in_specs=[vmem] * 4, out_sp...  3.66 us

profile of v2, /device:TPU:1, one launch (start us, length us, event | category | flops | bytes accessed | tf_op | source)
XLA Modules:
  0.0 86.4 jit_solution(6266052931649449220)
XLA Ops:
  0.6 82.1 %layer.1 = (bf16[32,128,128]{2,1,0:T(8,128)(2,1)}, bf16[4096,256]{1,0:T(8,128)(2,1)}, f32[256,128]{1,0:T(8,128)}, f32[256,128]{1,0:T(8,128)}) custom-call(s32[2,192]{1,0:T(2,128)} %bitcast.11, s32[8,256]{1,0:T(8,128)} %bitcast.10, s32[1,256]{1,0:T(1,128)} %count.1, bf16[4096,256]{1,0:T(8,128)(2,1)} %features_h.1, bf16[192,128,128]{2,1,0:T(8,128)(2,1)} %adjacency_h.1, ...), custom_call_target="tpu_custom_call" | custom-call | tf_op jit(solution)/shard_map/layer/pallas_call | solution.py:519
  82.7 3.7 %finish.1 = (bf16[32,128,128]{2,1,0:T(8,128)(2,1)}, bf16[4096,256]{1,0:T(8,128)(2,1)}, f32[256,128]{1,0:T(8,128)}, f32[256,128]{1,0:T(8,128)}) custom-call(bf16[32,128,128]{2,1,0:T(8,128)(2,1)} %get-tuple-element.12.act, bf16[4096,256]{1,0:T(8,128)(2,1)} %get-tuple-element.13.gfeat, f32[256,128]{1,0:T(8,128)} %get-tuple-element.14.gself, ...), custom_call_target="tpu_custom_call" | custom-call | tf_op jit(solution)/shard_map/finish/pallas_call | solution.py:566

commit v3 on v2

--- a/solution.py
+++ b/solution.py
@@ -89,12 +89,12 @@
     mate = (dom + 1 - 2 * core, x)
 
     def xy_peer(k):
-        py = (y + k // NX) % NY
-        px = (x + k % NX) % NX
+        py = lax.rem(y + k // NX, NY)
+        px = lax.rem(x + k % NX, NX)
         return (z * NY + py) * 2 + core, px, py * NX + px
 
     def z_peer(dz):
-        pz = (z + dz) % NZ
+        pz = lax.rem(z + dz, NZ)
         return ((pz * NY + y) * 2 + core, x), pz
 
     barrier = pltpu.get_barrier_semaphore()
@@ -178,15 +178,12 @@
         second = jnp.where(core == 0, theirs, mine)
         send[i] = jnp.concatenate([first, second], axis=1).astype(BF16)
 
-        def go(k, carry):
+        for k in range(1, NXY):
             pdom, px, pxy = xy_peer(k)
             pltpu.make_async_remote_copy(
                 send.at[i, pxy], mid.at[i, xy], xy_send.at[lane, i], xy_recv.at[lane, i],
                 device_id=(pdom, px), device_id_type=MESH,
             ).start()
-            return carry
-
-        lax.fori_loop(1, NXY, go, 0)
         mid[i, xy] = send[i, xy]
 
     def wait_bytes(ref, sem):
@@ -202,13 +199,18 @@
         wait_bytes(mid.at[i, pl.ds(0, NXY - 1)], xy_recv.at[lane, i])
         wait_bytes(send.at[i, pl.ds(0, NXY - 1)], xy_send.at[lane, i])
 
-        @pl.when(i < NZ - 1)
-        def _():
+        if isinstance(i, int) and i < NZ - 1:
             z_copy(i, mid, land, lane).start()
-
-        @pl.when(i == NZ - 1)
-        def _():
+        elif isinstance(i, int):
             pltpu.make_async_copy(mid.at[i], land.at[z], own_sems.at[lane]).start()
+        else:
+            @pl.when(i < NZ - 1)
+            def _():
+                z_copy(i, mid, land, lane).start()
+
+            @pl.when(i == NZ - 1)
+            def _():
+                pltpu.make_async_copy(mid.at[i], land.at[z], own_sems.at[lane]).start()
 
     def finish_z(i, mid, land, lane):
         @pl.when(i < NZ - 1)
@@ -311,46 +313,39 @@
     def gather_plane(s, carry):
         pz = (z + step_offset(s)) % NZ
 
-        def pick(q, carry):
+        for q in range(2 * NXY):
             d = pz * 2 * NXY + (q // 8) * 8 + (q % 2) * 4 + (q // 2) % 4
             for j in range(CAP):
-                rows_f[pl.ds(q * CAP + j, 1), :] = gmean[pl.ds(slot_s[j, d], 1), :]
-            return carry
-
-        lax.fori_loop(0, 2 * NXY, pick, 0, unroll=16)
+                rows_f[q * CAP + j:q * CAP + j + 1, :] = gmean[pl.ds(slot_s[j, d], 1), :]
         start_swap(s, rows_f[...].reshape(NXY, 2, CAP, BLOCK), keep2, pass2, mate2, 1)
         return carry
 
     def send_back(s, carry):
         gather_plane(s, 0)
 
-        @pl.when(s >= 2)
+        @pl.when(s >= 3)
         def _():
-            start_xy(s - 2, keep2, pass2, mate2, send2, mid2, 1)
-
-        @pl.when(s >= 5)
-        def _():
-            start_z(s - 5, send2, mid2, land2, 1)
+            start_xy(s - 3, keep2, pass2, mate2, send2, mid2, 1)
 
         return carry
 
     lax.fori_loop(0, NZ, send_back, 0)
-    start_xy(NZ - 2, keep2, pass2, mate2, send2, mid2, 1)
-
     def transpose(b, carry):
         at = pl.ds(pl.multiple_of(b * BLOCK, BLOCK), BLOCK)
         gproj_t[:, at] = gpre[b].astype(F32).T.astype(BF16)
         slots_t[b] = gmean[pl.ds(b * BLOCK, BLOCK), :].T.astype(BF16)
         return carry
 
-    lax.fori_loop(0, OWN_BLOCKS // 2, transpose, 0, unroll=2)
-    start_xy(NZ - 1, keep2, pass2, mate2, send2, mid2, 1)
-    start_z(NZ - 5, send2, mid2, land2, 1)
-    start_z(NZ - 4, send2, mid2, land2, 1)
-    lax.fori_loop(OWN_BLOCKS // 2, OWN_BLOCKS, transpose, 0, unroll=2)
-    start_z(NZ - 3, send2, mid2, land2, 1)
-    start_z(NZ - 2, send2, mid2, land2, 1)
-    start_z(NZ - 1, send2, mid2, land2, 1)
+    for k in range(3):
+        start_xy(NZ - 3 + k, keep2, pass2, mate2, send2, mid2, 1)
+        start_z(k, send2, mid2, land2, 1)
+    lax.fori_loop(0, OWN_BLOCKS // 2, transpose, 0, unroll=4)
+    start_z(3, send2, mid2, land2, 1)
+    start_z(4, send2, mid2, land2, 1)
+    lax.fori_loop(OWN_BLOCKS // 2, OWN_BLOCKS, transpose, 0, unroll=4)
+    start_z(5, send2, mid2, land2, 1)
+    start_z(6, send2, mid2, land2, 1)
+    start_z(7, send2, mid2, land2, 1)
     gself = jnp.dot(gproj_t[...], feat[...], preferred_element_type=F32).T
 
     def wait_both(ref, lane, k):
@@ -358,15 +353,12 @@
         wait_bytes(ref, red_send.at[lane, k])
 
     def around_xy(src, dst, lane, k):
-        def go(j, carry):
+        for j in range(1, NXY):
             pdom, px, pxy = xy_peer(j)
             pltpu.make_async_remote_copy(
                 src(pxy), dst, red_send.at[lane, k], red_recv.at[lane, k],
                 device_id=(pdom, px), device_id_type=MESH,
             ).start()
-            return carry
-
-        lax.fori_loop(1, NXY, go, 0)
 
     def swap_sums(lane):
         return pltpu.make_async_remote_copy(
@@ -386,15 +378,12 @@
             value = value + xy_r[lane, k]
         sum_xy[lane] = value
 
-        def go(dz, carry):
+        for dz in range(1, NZ):
             peer, _ = z_peer(dz)
             pltpu.make_async_remote_copy(
                 sum_xy.at[lane], z_r.at[lane, z], red_send.at[lane, 1], red_recv.at[lane, 1],
                 device_id=peer, device_id_type=MESH,
             ).start()
-            return carry
-
-        lax.fori_loop(1, NZ, go, 0)
         z_r[lane, z] = value
 
     def reduce_2(lane):
@@ -482,17 +471,26 @@
     give_feat.wait()
 
 
-def finish_kernel(act, gfeat, gself, gneigh, act_out, gfeat_out, gself_out, gneigh_out, sems):
-    copies = [
-        pltpu.make_async_copy(src, dst, sems.at[k])
-        for k, (src, dst) in enumerate(
-            ((gfeat, gfeat_out), (act, act_out), (gself, gself_out), (gneigh, gneigh_out))
-        )
-    ]
-    for copy in copies:
-        copy.start()
-    for copy in copies:
-        copy.wait()
+def finish_kernel(act, gfeat, gself, gneigh, act_out, gfeat_out, gself_out, gneigh_out, act_v, gfeat_v, gself_v, gneigh_v, load, give):
+    copies = []
+    for src, mid, dst, cuts in (
+        (gfeat, gfeat_v, gfeat_out, 4), (act, act_v, act_out, 2), (gself, gself_v, gself_out, 1), (gneigh, gneigh_v, gneigh_out, 1)
+    ):
+        rows = src.shape[0] // cuts
+        for k in range(cuts):
+            at = pl.ds(k * rows, rows)
+            n = len(copies)
+            copies.append((
+                pltpu.make_async_copy(src.at[at], mid.at[at], load.at[n]),
+                pltpu.make_async_copy(mid.at[at], dst.at[at], give.at[n]),
+            ))
+    for into, _ in copies:
+        into.start()
+    for into, out in copies:
+        into.wait()
+        out.start()
+    for _, out in copies:
+        out.wait()
 
 
 def per_device(
@@ -566,9 +564,13 @@
     act, gfeat, gself, gneigh = pl.pallas_call(
         finish_kernel,
         out_shape=outs,
-        in_specs=[vmem] * 4,
+        in_specs=[hbm] * 4,
         out_specs=(hbm,) * 4,
-        scratch_shapes=[dma((4,))],
+        scratch_shapes=[
+            V((OWN_BLOCKS, BLOCK, BLOCK), BF16), V((ROOTS, 2 * BLOCK), BF16),
+            V((2 * BLOCK, BLOCK), F32), V((2 * BLOCK, BLOCK), F32), dma((8,)), dma((8,)),
+        ],
+        compiler_params=pltpu.CompilerParams(vmem_limit_bytes=60 << 20),
         name="finish",
     )(*results)
     return act.reshape(ROOTS, BLOCK), gfeat, gself, gneigh

time: 86.5 us -> 83.9 us (0.970)
  Pallas kernels: 85.8 us -> 83.1 us
    pallas_call x1, Pallas kernels: 82.1 us -> 80.2 us  [per_device(): pl.pallas_call(main_kernel, out_shape=outs, in_specs=[vmem, vmem, vmem, h...]
where the time goes in v3:
time: 83.9 us; the launch traced here: 83.7 us
  Pallas kernels  83.1 us (99%)
    pallas_call x1, Pallas kernels, per_device(): pl.pallas_call(main_kernel, out_shape=outs, in_specs=[vmem, vmem, vmem, h...  80.2 us
    pallas_call x1, Pallas kernels, per_device(): pl.pallas_call(finish_kernel, out_shape=outs, in_specs=[hbm] * 4, out_spe...  2.92 us

profile of v3, /device:TPU:1, one launch (start us, length us, event | category | flops | bytes accessed | tf_op | source)
XLA Modules:
  0.0 83.7 jit_solution(17612985721798592086)
XLA Ops:
  0.6 80.2 %layer.1 = (bf16[32,128,128]{2,1,0:T(8,128)(2,1)}, bf16[4096,256]{1,0:T(8,128)(2,1)}, f32[256,128]{1,0:T(8,128)}, f32[256,128]{1,0:T(8,128)}) custom-call(s32[2,192]{1,0:T(2,128)} %bitcast.11, s32[8,256]{1,0:T(8,128)} %bitcast.10, s32[1,256]{1,0:T(1,128)} %count.1, bf16[4096,256]{1,0:T(8,128)(2,1)} %features_h.1, bf16[192,128,128]{2,1,0:T(8,128)(2,1)} %adjacency_h.1, ...), custom_call_target="tpu_custom_call" | custom-call | tf_op jit(solution)/shard_map/layer/pallas_call | solution.py:517
  80.8 2.9 %finish.1 = (bf16[32,128,128]{2,1,0:T(8,128)(2,1)}, bf16[4096,256]{1,0:T(8,128)(2,1)}, f32[256,128]{1,0:T(8,128)}, f32[256,128]{1,0:T(8,128)}) custom-call(bf16[32,128,128]{2,1,0:T(8,128)(2,1)} %get-tuple-element.12.act, bf16[4096,256]{1,0:T(8,128)(2,1)} %get-tuple-element.13.gfeat, f32[256,128]{1,0:T(8,128)} %get-tuple-element.14.gself, ...), custom_call_target="tpu_custom_call" | custom-call | tf_op jit(solution)/shard_map/finish/pallas_call | solution.py:564

commit v4 on v3

--- a/solution.py
+++ b/solution.py
@@ -154,7 +154,7 @@
         scan[i] = acc
         return acc
 
-    lax.fori_loop(0, TILES, forward, jnp.zeros((BLOCK, BLOCK), F32), unroll=24)
+    lax.fori_loop(0, TILES, forward, jnp.zeros((BLOCK, BLOCK), F32), unroll=48)
 
     pl.semaphore_wait(barrier, 1 + (NXY - 1) + (NZ - 1))
 
@@ -294,7 +294,7 @@
         gmean[pl.ds(b * BLOCK, BLOCK), :] = full * scale[b]
         return carry
 
-    lax.fori_loop(0, OWN_BLOCKS, activate, 0, unroll=2)
+    lax.fori_loop(0, OWN_BLOCKS, activate, 0, unroll=4)
     give_act = pltpu.make_async_copy(act, act_out, out_sems.at[0])
     give_act.start()
     gmean[pl.ds(ROOTS, CAP), :] = jnp.zeros((CAP, BLOCK), F32)
@@ -434,7 +434,7 @@
         scan[i] = acc
         return acc
 
-    lax.fori_loop(0, MOST_CLONE, back_clone, jnp.zeros((BLOCK, BLOCK), F32), unroll=20)
+    lax.fori_loop(0, MOST_CLONE, back_clone, jnp.zeros((BLOCK, BLOCK), F32), unroll=40)
 
     def gather_proj(c, carry):
         value = total[c] + scan[table[LAST_BWD, OWN_BLOCKS + c]]
@@ -442,7 +442,7 @@
         gproj_t[:, at] = value.astype(BF16)
         return carry
 
-    lax.fori_loop(0, OWN_BLOCKS, gather_proj, 0, unroll=4)
+    lax.fori_loop(0, OWN_BLOCKS, gather_proj, 0, unroll=16)
     reduce_2(0)
     gneigh = jnp.dot(gproj_t[...], feat[...], preferred_element_type=F32).T
 

time: 83.9 us -> 83.8 us (level)
  no operation moved by 1% of the time
where the time goes in v4:
time: 83.8 us; the launch traced here: 83.7 us
  Pallas kernels  83 us (99%)
    pallas_call x1, Pallas kernels, per_device(): pl.pallas_call(main_kernel, out_shape=outs, in_specs=[vmem, vmem, vmem, h...  80.1 us
    pallas_call x1, Pallas kernels, per_device(): pl.pallas_call(finish_kernel, out_shape=outs, in_specs=[hbm] * 4, out_spe...  2.92 us

profile of v4, /device:TPU:1, one launch (start us, length us, event | category | flops | bytes accessed | tf_op | source)
XLA Modules:
  0.0 83.7 jit_solution(5565189925259392804)
XLA Ops:
  0.6 80.1 %layer.1 = (bf16[32,128,128]{2,1,0:T(8,128)(2,1)}, bf16[4096,256]{1,0:T(8,128)(2,1)}, f32[256,128]{1,0:T(8,128)}, f32[256,128]{1,0:T(8,128)}) custom-call(s32[2,192]{1,0:T(2,128)} %bitcast.11, s32[8,256]{1,0:T(8,128)} %bitcast.10, s32[1,256]{1,0:T(1,128)} %count.1, bf16[4096,256]{1,0:T(8,128)(2,1)} %features_h.1, bf16[192,128,128]{2,1,0:T(8,128)(2,1)} %adjacency_h.1, ...), custom_call_target="tpu_custom_call" | custom-call | tf_op jit(solution)/shard_map/layer/pallas_call | solution.py:517
  80.7 2.9 %finish.1 = (bf16[32,128,128]{2,1,0:T(8,128)(2,1)}, bf16[4096,256]{1,0:T(8,128)(2,1)}, f32[256,128]{1,0:T(8,128)}, f32[256,128]{1,0:T(8,128)}) custom-call(bf16[32,128,128]{2,1,0:T(8,128)(2,1)} %get-tuple-element.12.act, bf16[4096,256]{1,0:T(8,128)(2,1)} %get-tuple-element.13.gfeat, f32[256,128]{1,0:T(8,128)} %get-tuple-element.14.gself, ...), custom_call_target="tpu_custom_call" | custom-call | tf_op jit(solution)/shard_map/finish/pallas_call | solution.py:564
